TPU v7x, 32 devices: a whole 2x2x4 slice. The times are simulated.
32 devices in a mesh: groups: 2 (over x), row: 16 (over z, y, core).
Axes of the slice: x: 2, y: 2, z: 4, core: 2. Of those that a mesh axis runs over, the one named last changes fastest.
Arguments:
- amplitudes: bfloat16 [256, 16384], P(('groups', 'row')), parts along dimension 0, may hold values from -6 to 6
- integrals: bfloat16 [16384, 2048], P('row', 'groups'), parts along dimension 1, may hold values from -0.09375 to 0.09375
- constant: float32 [128, 2048], P('row', 'groups'), parts along dimension 1, may hold values from -4 to 4
- occ_pairs: int32 [256, 2], P(('groups', 'row')), parts along dimension 0, may hold values from 0 to 239
- batch_pairs: int32 [2048, 2], P('groups'), parts along dimension 0, may hold values from 0 to 1599
- occ_irrep: int32 [480], P('groups'), parts along dimension 0, may hold values from 0 to 7
- vir_irrep: int32 [3200], P('groups'), parts along dimension 0, may hold values from 0 to 7
- occ_energy: float32 [480], P('groups'), parts along dimension 0, may hold values from -1.5 to -0.3
- vir_energy: float32 [3200], P('groups'), parts along dimension 0, may hold values from 0.2 to 1.5
- t2_pattern: int32 [8, 512], P(None, 'groups'), parts along dimension 1, may hold values 0 or 1
- int_pattern: int32 [512, 8], P(('groups', 'row')), parts along dimension 0, may hold values 0 or 1
Outputs:
- new_amplitudes: float32 [128, 2048], P('row', 'groups'), parts along dimension 1
There are 2 independent parts, one for each index of `groups`. A program takes and returns all parts, laid end to end along the dimension named above; each array names one. Nothing has to cross between parts.
All inputs are finite; a program needn't handle non-finite values. No bound on the sum of `int_pattern` on one device may be relied on, other than what follows from the above.
Results may differ from a plain program's by a relative error of at most 0.0003.
Values may be sent and summed in bfloat16 or wider, within the bound.
A program may use at most 64 MiB of HBM per device.

v0:
```python
import jax
import jax.numpy as jnp
from jax import lax
from jax.sharding import PartitionSpec as P

IRREPS = 8
BLOCK = 64


def lookup(table, index):
    places = jnp.arange(table.shape[0], dtype=jnp.int32)
    return jnp.sum(
        jnp.where(index[:, None] == places[None, :], table[None, :], jnp.zeros((), table.dtype)),
        axis=1,
    )


def per_device(
    amplitudes,
    integrals,
    constant,
    occ_pairs,
    batch_pairs,
    occ_irrep,
    vir_irrep,
    occ_energy,
    vir_energy,
    t2_pattern,
    int_pattern,
):
    labels = jnp.arange(IRREPS, dtype=jnp.int32)
    pair_irrep = jnp.bitwise_xor(
        lookup(occ_irrep, occ_pairs[:, 0]), lookup(occ_irrep, occ_pairs[:, 1])
    )
    batch_irrep = jnp.bitwise_xor(
        lookup(vir_irrep, batch_pairs[:, 0]), lookup(vir_irrep, batch_pairs[:, 1])
    )
    row_pattern = jnp.sum(
        jnp.where(pair_irrep[:, None, None] == labels[None, :, None], t2_pattern[None, :, :], 0),
        axis=1,
    )
    amask = jnp.repeat(row_pattern, BLOCK, axis=1)
    masked_amps = jnp.where(amask != 0, amplitudes, jnp.zeros((), jnp.bfloat16))
    col_pattern = jnp.sum(
        jnp.where(batch_irrep[None, None, :] == labels[None, :, None], int_pattern[:, :, None], 0),
        axis=1,
    )
    imask = jnp.repeat(col_pattern, BLOCK, axis=0)
    masked_ints = jnp.where(imask != 0, integrals, jnp.zeros((), jnp.bfloat16))
    gathered = lax.all_to_all(masked_amps, "row", split_axis=1, concat_axis=0, tiled=True)
    share = lax.psum_scatter(
        jnp.dot(gathered, masked_ints, preferred_element_type=jnp.float32),
        "row",
        scatter_dimension=0,
        tiled=True,
    )
    occ_sum = lookup(occ_energy, occ_pairs[:, 0]) + lookup(occ_energy, occ_pairs[:, 1])
    vir_sum = lookup(vir_energy, batch_pairs[:, 0]) + lookup(vir_energy, batch_pairs[:, 1])
    denom = vir_sum[None, :] - occ_sum[:, None]
    return (constant + share) / denom


def solution(mesh):
    in_specs = (
        P(("groups", "row"), None),
        P("row", "groups"),
        P("row", "groups"),
        P(("groups", "row"), None),
        P("groups", None),
        P("groups"),
        P("groups"),
        P("groups"),
        P("groups"),
        P(None, "groups"),
        P(("groups", "row"), None),
    )
    out_specs = P("row", "groups")
    return jax.shard_map(
        per_device, mesh=mesh, in_specs=in_specs, out_specs=out_specs, check_vma=False
    )
```

profile of v0, /device:TPU:0, one launch (start us, length us, event | category | flops | bytes accessed | tf_op | source)
XLA Modules:
  0.0 92.8 jit_solution(4269926450533298919)
XLA Ops:
  6.5 0.8 slice_bitcast_fusion.1
  7.3 0.9 select_reduce_fusion.8
  8.2 0.1 iota_compare_fusion.5
  8.3 0.8 select_reduce_fusion.5
  9.1 0.3 broadcast_in_dim.147
  9.4 0.5 ne.22
  9.9 1.7 %broadcast_select_fusion = bf16[8,16384]{1,0:T(8,128)(2,1)} fusion(pred[8,16384]{1,0:T(8,128)(4,1)S(1)} %ne.22, bf16[8,16384]{1,0:T(8,128)(2,1)} %param.11), kind=kLoop, calls=%fused_computation.10 | loop fusion | flops 131072 | bytes 655360 | tf_op jit(solution)/shard_map/jit(_where)/select_n | solution.py:43
  11.6 7.4 %all-to-all-start = ((bf16[8,16,1024]{2,0,1:T(8,128)(2,1)}), bf16[8,16,1024]{2,0,1:T(8,128)(2,1)S(1)}, u32[]{:S(2)}, u32[]{:S(2)}) async-start(bf16[8,16,1024]{2,0,1:T(8,128)(2,1)} %bitcast.2), calls=%async_computation | async-start | bytes 524288 | tf_op jit(solution)/shard_map/all_to_all | solution.py:50
  19.0 0.0 reduce-scatter.2.cloned.1.call-start
  19.0 0.8 copy.14
  19.8 0.8 fusion.2
  20.6 2.4 %select_reduce_fusion.2 = (s32[1024]{0:T(1024)S(1)}, s32[1024]{0:T(1024)S(1)}) fusion(s32[1024]{0:T(1024)S(1)} %bitcast.17, s32[1600]{0:T(1024)} %param.17, s32[1024]{0:T(1024)S(1)} %bitcast.15), kind=kLoop, calls=%fused_computation.2 | loop fusion | flops 9828352 | bytes 22784 | tf_op jit(solution)/shard_map/reduce_sum | solution.py:12
  23.0 0.2 select_reduce_fusion.4
  23.2 1.8 %bitcast_select_fusion = bf16[1024,1024]{1,0:T(8,128)(2,1)S(1)} fusion(bf16[1024,1024]{1,0:T(8,128)(2,1)} %param.12, pred[16,1024]{1,0:T(8,128)(4,1)S(1)} %broadcast_compare_fusion), kind=kLoop, calls=%fused_computation.6 | loop fusion | flops 1048576 | bytes 4210688 | tf_op jit(solution)/shard_map/jit(_where)/select_n | solution.py:49
  25.0 0.0 copy-start.1
  25.0 0.0 copy-start.2
  25.0 0.0 copy-start
  25.0 4.0 %all-to-all-done = bf16[8,16,1024]{2,0,1:T(8,128)(2,1)S(1)} async-done(((bf16[8,16,1024]{2,0,1:T(8,128)(2,1)}), bf16[8,16,1024]{2,0,1:T(8,128)(2,1)S(1)}, u32[]{:S(2)}, u32[]{:S(2)}) %all-to-all-start) | async-done | bytes 262176 | tf_op jit(solution)/shard_map/all_to_all | solution.py:50
  29.0 1.2 %fusion = f32[128,1024]{1,0:T(8,128)} fusion(bf16[1024,1024]{1,0:T(8,128)(2,1)S(1)} %bitcast_select_fusion, bf16[8,16,1024]{2,0,1:T(8,128)(2,1)S(1)} %all-to-all-done), kind=kOutput, calls=%fused_computation.8 | convolution fusion | flops 268435456 | bytes 2883584 | tf_op jit(solution)/shard_map/dot_general | solution.py:52
  30.3 0.0 reduce-scatter.2.cloned.1.call-update
  30.3 0.2 select_reduce_fusion.6
  30.5 1.7 %select_reduce_fusion = (f32[1024]{0:T(1024)S(1)}, f32[1024]{0:T(1024)S(1)}) fusion(f32[1600]{0:T(1024)S(1)} %copy-done.2, s32[1024]{0:T(1024)S(1)} %bitcast.18, s32[1024]{0:T(1024)S(1)} %bitcast.16), kind=kLoop, calls=%fused_computation | loop fusion | flops 9828352 | bytes 22784 | tf_op jit(solution)/shard_map/reduce_sum | solution.py:12
  32.3 52.2 %reduce-scatter.2.cloned.1.call-done = f32[8,1024]{1,0:T(8,128)} async-done(((f32[128,1024]{1,0:T(8,128)}), f32[8,1024]{1,0:T(8,128)}) %reduce-scatter.2.cloned.1.call-update) | async-done | bytes 32784 | tf_op jit(solution)/shard_map/reduce_scatter | solution.py:51
  84.5 1.5 %subtract_divide_fusion = f32[8,1024]{1,0:T(8,128)} fusion(f32[8,1024]{1,0:T(8,128)S(1)} %copy-done, f32[8,1024]{1,0:T(8,128)} %reduce-scatter.2.cloned.1.call-done, f32[8]{0:T(128)S(1)} %add.21, f32[1024]{0:T(1024)S(1)} %add.20), kind=kLoop, calls=%fused_computation.12 | loop fusion | flops 24576 | bytes 102432 | tf_op jit(solution)/shard_map/div | solution.py:60
  (10 shorter events, 0.1 us)
Async XLA Ops:
  11.6 17.4 %all-to-all-start = ((bf16[8,16,1024]{2,0,1:T(8,128)(2,1)}), bf16[8,16,1024]{2,0,1:T(8,128)(2,1)S(1)}, u32[]{:S(2)}, u32[]{:S(2)}) async-start(bf16[8,16,1024]{2,0,1:T(8,128)(2,1)} %bitcast.2), calls=%async_computation | async-start | bytes 524288 | tf_op jit(solution)/shard_map/all_to_all | solution.py:50
  19.0 65.5 %reduce-scatter.2.cloned.1.call-start = ((), (), s32[]{:S(2)}) async-start(), calls=%async_computation.2 | async-start | bytes 557056 | tf_op jit(solution)/shard_map/reduce_scatter | solution.py:51
  25.0 5.3 %copy-start.1 = (f32[240]{0:T(256)S(1)}, f32[240]{0:T(256)}, u32[]{:S(2)}) copy-start(f32[240]{0:T(256)} %param.18) | copy-start | bytes 2884
  25.0 5.5 %copy-start.2 = (f32[1600]{0:T(1024)S(1)}, f32[1600]{0:T(1024)}, u32[]{:S(2)}) copy-start(f32[1600]{0:T(1024)} %param.19) | copy-start | bytes 19204
  25.0 59.5 %copy-start = (f32[8,1024]{1,0:T(8,128)S(1)}, f32[8,1024]{1,0:T(8,128)}, u32[]{:S(2)}) copy-start(f32[8,1024]{1,0:T(8,128)} %param.13) | copy-start | bytes 98308
Sparse Core Ops, SparseCore 0:
  30.4 54.0 reduce-scatter.1
where the time goes:
time: 93.4 us; the launch traced here: 92.8 us
  waiting for transfers between devices  56.2 us (60%)
  between operations  13.5 us (14%)
  other arithmetic  11.2 us (12%)
  starting transfers between devices  7.43 us (8%)
  local copies, waits for them, and re-layouts  3.14 us (3%)
  matrix products  1.24 us (1%)
    reduce_scatter x1, waiting for transfers between devices, per_device(): lax.psum_scatter(jnp.dot(gathered, masked_ints, preferred_element_type=jn...  52.2 us
    all_to_all x1, starting transfers between devices, per_device(): lax.all_to_all(masked_amps, 'row', split_axis=1, concat_axis=0, tiled=True)  7.39 us
    reduce_sum x4, other arithmetic, lookup(): jnp.sum(jnp.where(index[:, None] == places[None, :], table[None, :], jnp....  5.2 us
    all_to_all x1, waiting for transfers between devices, per_device(): lax.all_to_all(masked_amps, 'row', split_axis=1, concat_axis=0, tiled=True)  3.98 us
  transfers between devices with their start and end apart: 2, of which 2 were waited for; matrix products, arithmetic and copies ran while one was open for 8% of the time, Pallas kernels for 0%

commit v1 on v0

v1 whole, which is shorter than its diff:
```python
import functools

import jax
import jax.numpy as jnp
from jax import lax
from jax.experimental import pallas as pl
from jax.experimental.pallas import tpu as pltpu
from jax.sharding import PartitionSpec as P

IRREPS = 8
BLOCK = 64
LANES = 128
F32 = jnp.float32
BF16 = jnp.bfloat16


def iota(shape, axis):
    return lax.broadcasted_iota(jnp.int32, shape, axis)


def fold(x):
    half = x.shape[1] // 2
    return jnp.concatenate([x[:, :half], x[:, half:]], axis=0)


def kernel(
    n,
    amps_hbm,
    ints_hbm,
    const_ref,
    occ_pairs_ref,
    batch_pairs_ref,
    occ_irrep_ref,
    vir_irrep_ref,
    occ_energy_ref,
    vir_energy_ref,
    t2_ref,
    intp_ref,
    out_ref,
    amps,
    ints,
    pattern,
    outgoing,
    incoming,
    part,
    from_mate,
    wire_out,
    wire_in,
    local_sem,
    send_sem,
    recv_sem,
    mate_sem,
    wire_sem,
):
    me = lax.axis_index("row")
    chips = n // 2
    core = lax.rem(me, 2)
    chip = me // 2
    mate = me + 1 - 2 * core
    rows = amps.shape[0]
    depth = ints.shape[0]
    width = ints.shape[1]

    barrier = pltpu.get_barrier_semaphore()

    def greet(k, carry):
        pl.semaphore_signal(barrier, inc=1, device_id={"row": lax.rem(me + k, n)}, device_id_type=pl.DeviceIdType.MESH)
        return carry

    get_amps = pltpu.make_async_copy(amps_hbm, amps, local_sem.at[0])
    get_ints = pltpu.make_async_copy(ints_hbm, ints, local_sem.at[1])
    get_amps.start()
    lax.fori_loop(1, n, greet, 0)
    get_ints.start()

    nocc = occ_irrep_ref.shape[1]
    places = iota((rows, nocc), 1)
    first = occ_pairs_ref[:, 0:1] == places
    second = occ_pairs_ref[:, 1:2] == places
    irr = occ_irrep_ref[...]
    en = occ_energy_ref[...]
    pair_irrep = jnp.bitwise_xor(
        jnp.sum(jnp.where(first, irr, 0), axis=1, keepdims=True),
        jnp.sum(jnp.where(second, irr, 0), axis=1, keepdims=True),
    )
    occ_sum = jnp.sum(jnp.where(first, en, 0.0), axis=1, keepdims=True) + jnp.sum(
        jnp.where(second, en, 0.0), axis=1, keepdims=True
    )

    kept = jnp.zeros((rows, t2_ref.shape[1]), jnp.int32)
    for label in range(IRREPS):
        kept = jnp.where(pair_irrep == label, t2_ref[label : label + 1, :], kept)
    pattern[...] = jnp.where(kept != 0, 1.0, 0.0)
    blocks = depth // BLOCK
    per_tile = LANES // blocks
    spread = jnp.where(iota((LANES, depth), 0) == iota((LANES, depth), 1) // BLOCK, 1.0, 0.0).astype(BF16)
    get_amps.wait()

    def mask_tile(tile, carry):
        block_rows = pattern[:, pl.ds(pl.multiple_of(tile * LANES, LANES), LANES)]
        turned = [
            block_rows if k == 0 else pltpu.roll(block_rows, LANES - k * blocks, 1) for k in range(per_tile)
        ]
        mask = jnp.dot(jnp.concatenate(turned, axis=0).astype(BF16), spread, preferred_element_type=F32)
        for k in range(per_tile):
            first_col = pl.multiple_of((tile * per_tile + k) * depth, LANES)
            values = amps[:, pl.ds(first_col, depth)].astype(F32)
            values = jnp.where(mask[k * rows : (k + 1) * rows] != 0.0, values, 0.0)
            outgoing[tile * per_tile + k] = fold(values).astype(BF16)
        return carry

    lax.fori_loop(0, n // per_tile, mask_tile, 0)
    incoming[core * chips + chip] = outgoing[me]

    pl.semaphore_wait(barrier, n - 1)

    def amps_copy(target, parity):
        return pltpu.make_async_remote_copy(
            src_ref=outgoing.at[target],
            dst_ref=incoming.at[core * chips + chip],
            send_sem=send_sem.at[parity],
            recv_sem=recv_sem.at[parity],
            device_id={"row": target},
            device_id_type=pl.DeviceIdType.MESH,
        )

    def send_unlike(k, carry):
        amps_copy(2 * lax.rem(chip + k, chips) + 1 - core, 0).start()
        return carry

    def send_like(k, carry):
        amps_copy(2 * lax.rem(chip + k, chips) + core, 1).start()
        return carry

    lax.fori_loop(0, chips, send_unlike, 0)
    lax.fori_loop(1, chips, send_like, 0)

    nvir = vir_irrep_ref.shape[1]
    highs = -(-nvir // LANES)
    high_rows = -(-highs // 8) * 8

    def table(ref):
        full = nvir // LANES
        pieces = [ref[:, i * LANES : (i + 1) * LANES].astype(F32) for i in range(full)]
        if nvir % LANES:
            rest = ref[:, full * LANES : nvir].astype(F32)
            pieces.append(jnp.concatenate([rest, jnp.zeros((1, LANES - nvir % LANES), F32)], axis=1))
        if high_rows > highs:
            pieces.append(jnp.zeros((high_rows - highs, LANES), F32))
        return jnp.concatenate(pieces, axis=0)

    energies = table(vir_energy_ref)
    top = energies.astype(BF16)
    rest = energies - top.astype(F32)
    middle = rest.astype(BF16)
    last = (rest - middle.astype(F32)).astype(BF16)
    tables = jnp.concatenate([table(vir_irrep_ref).astype(BF16), top, middle, last], axis=0)

    def batch_lookup(row):
        index = batch_pairs_ref[row : row + 1, :]
        low = jnp.bitwise_and(index, LANES - 1)
        high = lax.shift_right_logical(index, 7)
        onehot = jnp.where(iota((LANES, width), 0) == low, 1.0, 0.0).astype(BF16)
        found = jnp.dot(tables, onehot, preferred_element_type=F32)
        pick = iota((high_rows, width), 0) == high
        label = jnp.sum(jnp.where(pick, found[:high_rows], 0.0), axis=0, keepdims=True)
        energy = found[high_rows : 2 * high_rows] + found[2 * high_rows : 3 * high_rows] + found[3 * high_rows :]
        return label.astype(jnp.int32), jnp.sum(jnp.where(pick, energy, 0.0), axis=0, keepdims=True)

    label_a, energy_a = batch_lookup(0)
    label_b, energy_b = batch_lookup(1)
    batch_irrep = jnp.bitwise_xor(label_a, label_b)
    denom = (energy_a + energy_b) - occ_sum

    kept = jnp.zeros((blocks, width), jnp.int32)
    for label in range(IRREPS):
        kept = jnp.where(batch_irrep == label, intp_ref[:, label : label + 1], kept)
    kept = jnp.where(kept != 0, 1.0, 0.0)
    get_ints.wait()
    for b in range(blocks):
        keep = jnp.broadcast_to(kept[b : b + 1], (16, width)).astype(BF16)
        for i in range(BLOCK // 16):
            at = b * BLOCK + i * 16
            ints[at : at + 16, :] = ints[at : at + 16, :] * keep

    group = min(chips, 8)
    half = depth // 2

    def multiply(parity):
        def step(g, carry):
            planes = incoming[pl.ds(parity * chips + g * group, group)].astype(F32)
            left = planes[:, :rows].reshape(group * rows, half).astype(BF16)
            right = planes[:, rows:].reshape(group * rows, half).astype(BF16)
            product = jnp.dot(left, ints[:half, :], preferred_element_type=F32) + jnp.dot(
                right, ints[half:, :], preferred_element_type=F32
            )
            part[parity, pl.ds(g * group, group)] = product.reshape(group, rows, width)
            return carry

        lax.fori_loop(0, chips // group, step, 0)

    def wait_planes(sem, count):
        planes = incoming.at[pl.ds(0, count)]
        pltpu.make_async_copy(planes, planes, sem).wait()

    wait_planes(recv_sem.at[0], chips)
    multiply(1 - core)
    to_mate = pltpu.make_async_remote_copy(
        src_ref=part.at[1 - core],
        dst_ref=from_mate,
        send_sem=mate_sem.at[0],
        recv_sem=mate_sem.at[1],
        device_id={"row": mate},
        device_id_type=pl.DeviceIdType.MESH,
    )
    to_mate.start()
    wait_planes(recv_sem.at[1], chips - 1)
    multiply(core)
    to_mate.wait_recv()

    def wire_copy(target):
        return pltpu.make_async_remote_copy(
            src_ref=wire_out.at[target],
            dst_ref=wire_in.at[chip],
            send_sem=wire_sem.at[0],
            recv_sem=wire_sem.at[1],
            device_id={"row": 2 * target + core},
            device_id_type=pl.DeviceIdType.MESH,
        )

    def send_sum(k, carry):
        target = lax.rem(chip + k, chips)
        wire_out[target] = part[core, target] + from_mate[target]
        wire_copy(target).start()
        return carry

    lax.fori_loop(1, chips, send_sum, 0)
    mine = const_ref[...] + part[core, chip] + from_mate[chip]

    arrived = wire_in.at[pl.ds(0, chips - 1)]
    pltpu.make_async_copy(arrived, arrived, wire_sem.at[1]).wait()

    def add(k, total):
        return total + wire_in[lax.rem(chip + k, chips)]

    total = lax.fori_loop(1, chips, add, mine)
    out_ref[...] = total / denom

    wait_planes(send_sem.at[0], chips)
    wait_planes(send_sem.at[1], chips - 1)
    to_mate.wait_send()
    sent = wire_out.at[pl.ds(0, chips - 1)]
    pltpu.make_async_copy(sent, sent, wire_sem.at[0]).wait()


def per_device(
    n,
    amplitudes,
    integrals,
    constant,
    occ_pairs,
    batch_pairs,
    occ_irrep,
    vir_irrep,
    occ_energy,
    vir_energy,
    t2_pattern,
    int_pattern,
):
    rows = amplitudes.shape[0]
    depth, width = integrals.shape
    chips = n // 2
    vmem = pl.BlockSpec(memory_space=pltpu.VMEM)
    hbm = pl.BlockSpec(memory_space=pl.ANY)
    return pl.pallas_call(
        functools.partial(kernel, n),
        out_shape=jax.ShapeDtypeStruct((rows, width), F32),
        in_specs=[hbm, hbm] + [vmem] * 9,
        out_specs=vmem,
        scratch_shapes=[
            pltpu.VMEM((rows, n * depth), BF16),
            pltpu.VMEM((depth, width), BF16),
            pltpu.VMEM((rows, t2_pattern.shape[1]), F32),
            pltpu.VMEM((n, 2 * rows, depth // 2), BF16),
            pltpu.VMEM((n, 2 * rows, depth // 2), BF16),
            pltpu.VMEM((2, chips, rows, width), F32),
            pltpu.VMEM((chips, rows, width), F32),
            pltpu.VMEM((chips, rows, width), F32),
            pltpu.VMEM((chips, rows, width), F32),
            pltpu.SemaphoreType.DMA((2,)),
            pltpu.SemaphoreType.DMA((2,)),
            pltpu.SemaphoreType.DMA((2,)),
            pltpu.SemaphoreType.DMA((2,)),
            pltpu.SemaphoreType.DMA((2,)),
        ],
        compiler_params=pltpu.CompilerParams(
            collective_id=0, has_side_effects=True, vmem_limit_bytes=60 * 1024 * 1024
        ),
        cost_estimate=pl.CostEstimate(
            flops=2 * n * rows * depth * width, bytes_accessed=2 * depth * width, transcendentals=0
        ),
    )(
        amplitudes,
        integrals,
        constant,
        occ_pairs,
        batch_pairs.T,
        occ_irrep[None, :],
        vir_irrep[None, :],
        occ_energy[None, :],
        vir_energy[None, :],
        t2_pattern,
        int_pattern,
    )


def solution(mesh):
    in_specs = (
        P(("groups", "row"), None),
        P("row", "groups"),
        P("row", "groups"),
        P(("groups", "row"), None),
        P("groups", None),
        P("groups"),
        P("groups"),
        P("groups"),
        P("groups"),
        P(None, "groups"),
        P(("groups", "row"), None),
    )
    out_specs = P("row", "groups")
    return jax.shard_map(
        functools.partial(per_device, mesh.shape["row"]),
        mesh=mesh,
        in_specs=in_specs,
        out_specs=out_specs,
        check_vma=False,
    )
```

time: 93.4 us -> 28.1 us (0.30)
  waiting for transfers between devices: 56.2 us -> 0 us
  Pallas kernels: 0 us -> 21.1 us
  between operations: 13.5 us -> 0.01 us
  other arithmetic: 11.2 us -> 0 us
  starting transfers between devices: 7.43 us -> 0 us
  local copies, waits for them, and re-layouts: 3.14 us -> 6.65 us
  matrix products: 1.24 us -> 0 us
    reduce_scatter x1 -> x0, waiting for transfers between devices: 52.2 us -> none  [per_device(): lax.psum_scatter(jnp.dot(gathered, masked_ints, preferred_element_type=jn...]
    pallas_call x0 -> x1, Pallas kernels: none -> 21.1 us  [per_device(): pl.pallas_call(functools.partial(kernel, n), out_shape=jax.ShapeDtypeStru...]
    all_to_all x1 -> x0, starting transfers between devices: 7.39 us -> none  [per_device(): lax.all_to_all(masked_amps, 'row', split_axis=1, concat_axis=0, tiled=True)]
    reduce_sum x6 -> x0, other arithmetic: 6.21 us -> none  [the longest x4 5.2 us: lookup(): jnp.sum(jnp.where(index[:, None] == places[None, :], table[None, :], jnp....]
    all_to_all x1 -> x0, waiting for transfers between devices: 3.98 us -> none  [per_device(): lax.all_to_all(masked_amps, 'row', split_axis=1, concat_axis=0, tiled=True)]
    select_n x2 -> x0, other arithmetic: 3.44 us -> none  [the longest x1 1.77 us: per_device(): masked_ints = jnp.where(imask != 0, integrals, jnp.zeros((), jnp.bfloat16))]
    unnamed x7 -> x3, local copies, waits for them, and re-layouts: 0.78 us -> 4.07 us
    broadcast_in_dim x1 -> x2, local copies, waits for them, and re-layouts: 0.34 us -> 2.58 us  [the longest x1 1.3 us: per_device(): vir_energy[None, :]]
  transfers between devices with their start and end apart: 2 -> 0, of which waited for: 2 -> 0; matrix products, arithmetic and copies ran while one was open for 8% -> 0% of each run, Pallas kernels for 0% -> 0%
where the time goes in v1:
time: 28.1 us; the launch traced here: 27.7 us
  Pallas kernels  21.1 us (75%)
  local copies, waits for them, and re-layouts  6.65 us (24%)
    pallas_call x1, Pallas kernels, per_device(): pl.pallas_call(functools.partial(kernel, n), out_shape=jax.ShapeDtypeStru...  21.1 us
    unnamed x3, local copies, waits for them, and re-layouts  4.07 us
    broadcast_in_dim x1, local copies, waits for them, and re-layouts, per_device(): vir_energy[None, :]  1.3 us
    broadcast_in_dim x1, local copies, waits for them, and re-layouts, per_device(): vir_irrep[None, :]  1.29 us

profile of v1, /device:TPU:0, one launch (start us, length us, event | category | flops | bytes accessed | tf_op | source)
XLA Modules:
  0.0 27.7 jit_solution(17415399187844125879)
XLA Ops:
  0.0 1.3 %copy.12.occ_pairs_ref = s32[8,2]{1,0:T(8,128)} copy(s32[8,2]{0,1:T(2,128)} %param.14) | data formatting | bytes 128 | tf_op args[3]
  1.3 1.3 %broadcast_in_dim.13.vir_irrep_ref = s32[1,1600]{1,0:T(1,128)} reshape(s32[1600]{0:T(1024)} %param.17) | data formatting | bytes 12800 | tf_op jit(solution)/shard_map/broadcast_in_dim | solution.py:309
  2.6 1.3 %broadcast_in_dim.15.vir_energy_ref = f32[1,1600]{1,0:T(1,128)} reshape(f32[1600]{0:T(1024)} %param.19) | data formatting | bytes 12800 | tf_op jit(solution)/shard_map/broadcast_in_dim | solution.py:311
  3.9 1.4 %copy.13.intp_ref = s32[16,8]{1,0:T(8,128)} copy(s32[16,8]{0,1:T(8,128)} %param.21) | data formatting | bytes 1024 | tf_op args[10]
  5.3 21.1 %shard_map.109 = f32[8,1024]{1,0:T(8,128)} custom-call(bf16[8,16384]{1,0:T(8,128)(2,1)} %amps_hbm.1, bf16[1024,1024]{1,0:T(8,128)(2,1)} %ints_hbm.1, f32[8,1024]{1,0:T(8,128)} %const_ref.1, s32[8,2]{1,0:T(8,128)} %copy.12.occ_pairs_ref, s32[2,1024]{1,0:T(2,128)} %bitcast.3, s32[1,240]{1,0:T(1,128)} %bitcast.4, s32[1,1600]{1,0:T(1,128)} %broadcast_in_dim.13.vir_irrep_ref, ...), custom_call_target="tpu_custom_call" | custom-call | flops 268435456 | bytes 2097152 | tf_op jit(solution)/shard_map/pallas_call | solution.py:275
  26.4 1.4 %copy.15 = f32[8,1024]{1,0:T(8,128)} copy(f32[8,1024]{1,0:T(8,128)} %shard_map.109) | data formatting | bytes 65536

commit v2 on v1

--- a/solution.py
+++ b/solution.py
@@ -21,6 +21,12 @@
 def fold(x):
     half = x.shape[1] // 2
     return jnp.concatenate([x[:, :half], x[:, half:]], axis=0)
+
+
+def upright(row):
+    k = row.shape[1]
+    square = jnp.broadcast_to(row, (k, k))
+    return jnp.sum(jnp.where(iota((k, k), 0) == iota((k, k), 1), square, jnp.zeros_like(square)), axis=1, keepdims=True)
 
 
 def kernel(
@@ -73,12 +79,12 @@
     lax.fori_loop(1, n, greet, 0)
     get_ints.start()
 
-    nocc = occ_irrep_ref.shape[1]
+    nocc = occ_irrep_ref.shape[0]
     places = iota((rows, nocc), 1)
-    first = occ_pairs_ref[:, 0:1] == places
-    second = occ_pairs_ref[:, 1:2] == places
-    irr = occ_irrep_ref[...]
-    en = occ_energy_ref[...]
+    first = upright(occ_pairs_ref[0:1, :]) == places
+    second = upright(occ_pairs_ref[1:2, :]) == places
+    irr = occ_irrep_ref[...].reshape(1, nocc)
+    en = occ_energy_ref[...].reshape(1, nocc)
     pair_irrep = jnp.bitwise_xor(
         jnp.sum(jnp.where(first, irr, 0), axis=1, keepdims=True),
         jnp.sum(jnp.where(second, irr, 0), axis=1, keepdims=True),
@@ -135,15 +141,15 @@
     lax.fori_loop(0, chips, send_unlike, 0)
     lax.fori_loop(1, chips, send_like, 0)
 
-    nvir = vir_irrep_ref.shape[1]
+    nvir = vir_irrep_ref.shape[0]
     highs = -(-nvir // LANES)
     high_rows = -(-highs // 8) * 8
 
     def table(ref):
         full = nvir // LANES
-        pieces = [ref[:, i * LANES : (i + 1) * LANES].astype(F32) for i in range(full)]
+        pieces = [ref[i * LANES : (i + 1) * LANES].reshape(1, LANES).astype(F32) for i in range(full)]
         if nvir % LANES:
-            rest = ref[:, full * LANES : nvir].astype(F32)
+            rest = ref[full * LANES : nvir].reshape(1, nvir - full * LANES).astype(F32)
             pieces.append(jnp.concatenate([rest, jnp.zeros((1, LANES - nvir % LANES), F32)], axis=1))
         if high_rows > highs:
             pieces.append(jnp.zeros((high_rows - highs, LANES), F32))
@@ -174,7 +180,7 @@
 
     kept = jnp.zeros((blocks, width), jnp.int32)
     for label in range(IRREPS):
-        kept = jnp.where(batch_irrep == label, intp_ref[:, label : label + 1], kept)
+        kept = jnp.where(batch_irrep == label, upright(intp_ref[label : label + 1, :]), kept)
     kept = jnp.where(kept != 0, 1.0, 0.0)
     get_ints.wait()
     for b in range(blocks):
@@ -303,14 +309,14 @@
         amplitudes,
         integrals,
         constant,
-        occ_pairs,
+        occ_pairs.T,
         batch_pairs.T,
-        occ_irrep[None, :],
-        vir_irrep[None, :],
-        occ_energy[None, :],
-        vir_energy[None, :],
+        occ_irrep,
+        vir_irrep,
+        occ_energy,
+        vir_energy,
         t2_pattern,
-        int_pattern,
+        int_pattern.T,
     )
 
 

time: 28.1 us -> 22.7 us (0.81)
  local copies, waits for them, and re-layouts: 6.65 us -> 1.38 us
    unnamed x3 -> x1, local copies, waits for them, and re-layouts: 4.07 us -> 1.38 us
    broadcast_in_dim x2 -> x0, local copies, waits for them, and re-layouts: 2.58 us -> none  [the longest x1 1.3 us: per_device(): vir_energy[None, :]]
where the time goes in v2:
time: 22.7 us; the launch traced here: 22.5 us
  Pallas kernels  21.1 us (93%)
  local copies, waits for them, and re-layouts  1.38 us (6%)
    pallas_call x1, Pallas kernels, per_device(): pl.pallas_call(functools.partial(kernel, n), out_shape=jax.ShapeDtypeStru...  21.1 us
    unnamed x1, local copies, waits for them, and re-layouts  1.38 us

profile of v2, /device:TPU:0, one launch (start us, length us, event | category | flops | bytes accessed | tf_op | source)
XLA Modules:
  0.0 22.5 jit_solution(18144030118350240877)
XLA Ops:
  0.0 21.1 %shard_map.109 = f32[8,1024]{1,0:T(8,128)} custom-call(bf16[8,16384]{1,0:T(8,128)(2,1)} %amps_hbm.1, bf16[1024,1024]{1,0:T(8,128)(2,1)} %ints_hbm.1, f32[8,1024]{1,0:T(8,128)} %const_ref.1, s32[2,8]{1,0:T(2,128)} %bitcast.5, s32[2,1024]{1,0:T(2,128)} %bitcast.3, s32[240]{0:T(256)} %occ_irrep_ref.1, s32[1600]{0:T(1024)} %vir_irrep_ref.1, f32[240]{0:T(256)} %occ_energy_ref.1, ...), custom_call_target="tpu_custom_call" | custom-call | flops 268435456 | bytes 2097152 | tf_op jit(solution)/shard_map/pallas_call | solution.py:281
  21.1 1.4 %copy.13 = f32[8,1024]{1,0:T(8,128)} copy(f32[8,1024]{1,0:T(8,128)} %shard_map.109) | data formatting | bytes 65536

commit v3 on v2

--- a/solution.py
+++ b/solution.py
@@ -12,6 +12,8 @@
 LANES = 128
 F32 = jnp.float32
 BF16 = jnp.bfloat16
+LEVELS = 32766.0
+TINY = 1e-30
 
 
 def iota(shape, axis):
@@ -21,12 +23,22 @@
 def fold(x):
     half = x.shape[1] // 2
     return jnp.concatenate([x[:, :half], x[:, half:]], axis=0)
+
+
+def unfold(x):
+    half = x.shape[0] // 2
+    return jnp.concatenate([x[:half], x[half:]], axis=1)
 
 
 def upright(row):
     k = row.shape[1]
     square = jnp.broadcast_to(row, (k, k))
     return jnp.sum(jnp.where(iota((k, k), 0) == iota((k, k), 1), square, jnp.zeros_like(square)), axis=1, keepdims=True)
+
+
+def flat(column):
+    k = column.shape[0]
+    return jnp.sum(jnp.where(iota((k, LANES), 0) == iota((k, LANES), 1), column, 0.0), axis=0, keepdims=True)
 
 
 def kernel(
@@ -52,6 +64,8 @@
     from_mate,
     wire_out,
     wire_in,
+    step_out,
+    step_in,
     local_sem,
     send_sem,
     recv_sem,
@@ -234,9 +248,23 @@
             device_id_type=pl.DeviceIdType.MESH,
         )
 
+    def step_copy(target):
+        return pltpu.make_async_remote_copy(
+            src_ref=step_out.at[target],
+            dst_ref=step_in.at[chip],
+            send_sem=wire_sem.at[2],
+            recv_sem=wire_sem.at[3],
+            device_id={"row": 2 * target + core},
+            device_id_type=pl.DeviceIdType.MESH,
+        )
+
     def send_sum(k, carry):
         target = lax.rem(chip + k, chips)
-        wire_out[target] = part[core, target] + from_mate[target]
+        both = part[core, target] + from_mate[target]
+        step = jnp.maximum(jnp.max(jnp.abs(both), axis=1, keepdims=True), TINY) * (1.0 / LEVELS)
+        step_out[target] = flat(step)
+        step_copy(target).start()
+        wire_out[target] = fold(jnp.round(both * (1.0 / step))).astype(jnp.int32).astype(jnp.int16)
         wire_copy(target).start()
         return carry
 
@@ -244,10 +272,14 @@
     mine = const_ref[...] + part[core, chip] + from_mate[chip]
 
     arrived = wire_in.at[pl.ds(0, chips - 1)]
+    steps_arrived = step_in.at[pl.ds(0, chips - 1)]
+    pltpu.make_async_copy(steps_arrived, steps_arrived, wire_sem.at[3]).wait()
     pltpu.make_async_copy(arrived, arrived, wire_sem.at[1]).wait()
 
     def add(k, total):
-        return total + wire_in[lax.rem(chip + k, chips)]
+        source = lax.rem(chip + k, chips)
+        codes = unfold(wire_in[source].astype(jnp.int32).astype(F32))
+        return total + codes * upright(step_in[source][:, :rows])
 
     total = lax.fori_loop(1, chips, add, mine)
     out_ref[...] = total / denom
@@ -257,6 +289,8 @@
     to_mate.wait_send()
     sent = wire_out.at[pl.ds(0, chips - 1)]
     pltpu.make_async_copy(sent, sent, wire_sem.at[0]).wait()
+    steps_sent = step_out.at[pl.ds(0, chips - 1)]
+    pltpu.make_async_copy(steps_sent, steps_sent, wire_sem.at[2]).wait()
 
 
 def per_device(
@@ -291,13 +325,15 @@
             pltpu.VMEM((n, 2 * rows, depth // 2), BF16),
             pltpu.VMEM((2, chips, rows, width), F32),
             pltpu.VMEM((chips, rows, width), F32),
-            pltpu.VMEM((chips, rows, width), F32),
-            pltpu.VMEM((chips, rows, width), F32),
+            pltpu.VMEM((chips, 2 * rows, width // 2), jnp.int16),
+            pltpu.VMEM((chips, 2 * rows, width // 2), jnp.int16),
+            pltpu.VMEM((chips, 1, LANES), F32),
+            pltpu.VMEM((chips, 1, LANES), F32),
             pltpu.SemaphoreType.DMA((2,)),
             pltpu.SemaphoreType.DMA((2,)),
             pltpu.SemaphoreType.DMA((2,)),
             pltpu.SemaphoreType.DMA((2,)),
-            pltpu.SemaphoreType.DMA((2,)),
+            pltpu.SemaphoreType.DMA((4,)),
         ],
         compiler_params=pltpu.CompilerParams(
             collective_id=0, has_side_effects=True, vmem_limit_bytes=60 * 1024 * 1024

time: 22.7 us -> 22.5 us (level)
  no operation moved by 1% of the time
where the time goes in v3:
time: 22.5 us; the launch traced here: 22.2 us
  Pallas kernels  20.9 us (93%)
  local copies, waits for them, and re-layouts  1.38 us (6%)
    pallas_call x1, Pallas kernels, per_device(): pl.pallas_call(functools.partial(kernel, n), out_shape=jax.ShapeDtypeStru...  20.9 us
    unnamed x1, local copies, waits for them, and re-layouts  1.38 us

profile of v3, /device:TPU:0, one launch (start us, length us, event | category | flops | bytes accessed | tf_op | source)
XLA Modules:
  0.0 22.2 jit_solution(7618285307075902247)
XLA Ops:
  0.0 20.9 %shard_map.109 = f32[8,1024]{1,0:T(8,128)} custom-call(bf16[8,16384]{1,0:T(8,128)(2,1)} %amps_hbm.1, bf16[1024,1024]{1,0:T(8,128)(2,1)} %ints_hbm.1, f32[8,1024]{1,0:T(8,128)} %const_ref.1, s32[2,8]{1,0:T(2,128)} %bitcast.5, s32[2,1024]{1,0:T(2,128)} %bitcast.3, s32[240]{0:T(256)} %occ_irrep_ref.1, s32[1600]{0:T(1024)} %vir_irrep_ref.1, f32[240]{0:T(256)} %occ_energy_ref.1, ...), custom_call_target="tpu_custom_call" | custom-call | flops 268435456 | bytes 2097152 | tf_op jit(solution)/shard_map/pallas_call | solution.py:315
  20.9 1.4 %copy.13 = f32[8,1024]{1,0:T(8,128)} copy(f32[8,1024]{1,0:T(8,128)} %shard_map.109) | data formatting | bytes 65536

commit v4 on v3

--- a/solution.py
+++ b/solution.py
@@ -25,11 +25,6 @@
     return jnp.concatenate([x[:, :half], x[:, half:]], axis=0)
 
 
-def unfold(x):
-    half = x.shape[0] // 2
-    return jnp.concatenate([x[:half], x[half:]], axis=1)
-
-
 def upright(row):
     k = row.shape[1]
     square = jnp.broadcast_to(row, (k, k))
@@ -37,14 +32,31 @@
 
 
 def flat(column):
-    k = column.shape[0]
-    return jnp.sum(jnp.where(iota((k, LANES), 0) == iota((k, LANES), 1), column, 0.0), axis=0, keepdims=True)
+    shape = column.shape[1], LANES
+    return jnp.sum(jnp.where((iota(shape, 0) == iota(shape, 1))[None], column, 0.0), axis=1, keepdims=True)
+
+
+def tall(row, k):
+    shape = k, LANES
+    return jnp.sum(jnp.where((iota(shape, 0) == iota(shape, 1))[None], row, 0.0), axis=2, keepdims=True)
 
 
 def kernel(
     n,
     amps_hbm,
     ints_hbm,
+    const_hbm,
+    occ_pairs_hbm,
+    batch_pairs_hbm,
+    occ_irrep_hbm,
+    vir_irrep_hbm,
+    occ_energy_hbm,
+    vir_energy_hbm,
+    t2_hbm,
+    intp_hbm,
+    out_ref,
+    amps,
+    ints,
     const_ref,
     occ_pairs_ref,
     batch_pairs_ref,
@@ -54,9 +66,6 @@
     vir_energy_ref,
     t2_ref,
     intp_ref,
-    out_ref,
-    amps,
-    ints,
     pattern,
     outgoing,
     incoming,
@@ -81,6 +90,7 @@
     depth = ints.shape[0]
     width = ints.shape[1]
 
+    unroll = n <= 16
     barrier = pltpu.get_barrier_semaphore()
 
     def greet(k, carry):
@@ -89,9 +99,25 @@
 
     get_amps = pltpu.make_async_copy(amps_hbm, amps, local_sem.at[0])
     get_ints = pltpu.make_async_copy(ints_hbm, ints, local_sem.at[1])
+    early = [(occ_pairs_hbm, occ_pairs_ref), (occ_irrep_hbm, occ_irrep_ref), (occ_energy_hbm, occ_energy_ref), (t2_hbm, t2_ref)]
+    late = [
+        (batch_pairs_hbm, batch_pairs_ref),
+        (vir_irrep_hbm, vir_irrep_ref),
+        (vir_energy_hbm, vir_energy_ref),
+        (intp_hbm, intp_ref),
+        (const_hbm, const_ref),
+    ]
+    get_early = [pltpu.make_async_copy(a, b, local_sem.at[2 + i]) for i, (a, b) in enumerate(early)]
+    get_late = [pltpu.make_async_copy(a, b, local_sem.at[6 + i]) for i, (a, b) in enumerate(late)]
+    for copy in get_early:
+        copy.start()
     get_amps.start()
-    lax.fori_loop(1, n, greet, 0)
+    lax.fori_loop(1, n, greet, 0, unroll=unroll)
+    for copy in get_late:
+        copy.start()
     get_ints.start()
+    for copy in get_early:
+        copy.wait()
 
     nocc = occ_irrep_ref.shape[0]
     places = iota((rows, nocc), 1)
@@ -152,9 +178,11 @@
         amps_copy(2 * lax.rem(chip + k, chips) + core, 1).start()
         return carry
 
-    lax.fori_loop(0, chips, send_unlike, 0)
-    lax.fori_loop(1, chips, send_like, 0)
-
+    lax.fori_loop(0, chips, send_unlike, 0, unroll=unroll)
+    lax.fori_loop(1, chips, send_like, 0, unroll=unroll)
+
+    for copy in get_late:
+        copy.wait()
     nvir = vir_irrep_ref.shape[0]
     highs = -(-nvir // LANES)
     high_rows = -(-highs // 8) * 8
@@ -258,30 +286,41 @@
             device_id_type=pl.DeviceIdType.MESH,
         )
 
+    def encode(g, carry):
+        some = pl.ds(g * group, group)
+        both = part[core, some] + from_mate[some]
+        step = jnp.maximum(jnp.max(jnp.abs(both), axis=2, keepdims=True), TINY) * (1.0 / LEVELS)
+        step_out[some] = flat(step)
+        codes = jnp.round(both * (1.0 / step))
+        codes = jnp.concatenate([codes[:, :, : width // 2], codes[:, :, width // 2 :]], axis=1)
+        wire_out[some] = codes.astype(jnp.int32).astype(jnp.int16)
+        return carry
+
     def send_sum(k, carry):
         target = lax.rem(chip + k, chips)
-        both = part[core, target] + from_mate[target]
-        step = jnp.maximum(jnp.max(jnp.abs(both), axis=1, keepdims=True), TINY) * (1.0 / LEVELS)
-        step_out[target] = flat(step)
         step_copy(target).start()
-        wire_out[target] = fold(jnp.round(both * (1.0 / step))).astype(jnp.int32).astype(jnp.int16)
         wire_copy(target).start()
         return carry
 
-    lax.fori_loop(1, chips, send_sum, 0)
-    mine = const_ref[...] + part[core, chip] + from_mate[chip]
+    lax.fori_loop(0, chips // group, encode, 0)
+    lax.fori_loop(1, chips, send_sum, 0, unroll=unroll)
+    step_in[chip] = step_out[chip]
+    wire_in[chip] = wire_out[chip]
 
     arrived = wire_in.at[pl.ds(0, chips - 1)]
     steps_arrived = step_in.at[pl.ds(0, chips - 1)]
     pltpu.make_async_copy(steps_arrived, steps_arrived, wire_sem.at[3]).wait()
     pltpu.make_async_copy(arrived, arrived, wire_sem.at[1]).wait()
 
-    def add(k, total):
-        source = lax.rem(chip + k, chips)
-        codes = unfold(wire_in[source].astype(jnp.int32).astype(F32))
-        return total + codes * upright(step_in[source][:, :rows])
-
-    total = lax.fori_loop(1, chips, add, mine)
+    def decode(g, total):
+        some = pl.ds(g * group, group)
+        step = tall(step_in[some], rows)
+        codes = wire_in[some].astype(jnp.int32).astype(F32)
+        left = jnp.sum(codes[:, :rows] * step, axis=0)
+        right = jnp.sum(codes[:, rows:] * step, axis=0)
+        return total + jnp.concatenate([left, right], axis=1)
+
+    total = lax.fori_loop(0, chips // group, decode, const_ref[...])
     out_ref[...] = total / denom
 
     wait_planes(send_sem.at[0], chips)
@@ -315,11 +354,20 @@
     return pl.pallas_call(
         functools.partial(kernel, n),
         out_shape=jax.ShapeDtypeStruct((rows, width), F32),
-        in_specs=[hbm, hbm] + [vmem] * 9,
+        in_specs=[hbm] * 11,
         out_specs=vmem,
         scratch_shapes=[
             pltpu.VMEM((rows, n * depth), BF16),
             pltpu.VMEM((depth, width), BF16),
+            pltpu.VMEM(constant.shape, F32),
+            pltpu.VMEM(occ_pairs.shape[::-1], jnp.int32),
+            pltpu.VMEM(batch_pairs.shape[::-1], jnp.int32),
+            pltpu.VMEM(occ_irrep.shape, jnp.int32),
+            pltpu.VMEM(vir_irrep.shape, jnp.int32),
+            pltpu.VMEM(occ_energy.shape, F32),
+            pltpu.VMEM(vir_energy.shape, F32),
+            pltpu.VMEM(t2_pattern.shape, jnp.int32),
+            pltpu.VMEM(int_pattern.shape[::-1], jnp.int32),
             pltpu.VMEM((rows, t2_pattern.shape[1]), F32),
             pltpu.VMEM((n, 2 * rows, depth // 2), BF16),
             pltpu.VMEM((n, 2 * rows, depth // 2), BF16),
@@ -329,7 +377,7 @@
             pltpu.VMEM((chips, 2 * rows, width // 2), jnp.int16),
             pltpu.VMEM((chips, 1, LANES), F32),
             pltpu.VMEM((chips, 1, LANES), F32),
-            pltpu.SemaphoreType.DMA((2,)),
+            pltpu.SemaphoreType.DMA((11,)),
             pltpu.SemaphoreType.DMA((2,)),
             pltpu.SemaphoreType.DMA((2,)),
             pltpu.SemaphoreType.DMA((2,)),

time: 22.5 us -> 21.3 us (0.947)
  Pallas kernels: 20.9 us -> 19.7 us
    pallas_call x1, Pallas kernels: 20.9 us -> 19.7 us  [per_device(): pl.pallas_call(functools.partial(kernel, n), out_shape=jax.ShapeDtypeStru...]
where the time goes in v4:
time: 21.3 us; the launch traced here: 21.1 us
  Pallas kernels  19.7 us (92%)
  local copies, waits for them, and re-layouts  1.38 us (6%)
    pallas_call x1, Pallas kernels, per_device(): pl.pallas_call(functools.partial(kernel, n), out_shape=jax.ShapeDtypeStru...  19.7 us
    unnamed x1, local copies, waits for them, and re-layouts  1.38 us

profile of v4, /device:TPU:0, one launch (start us, length us, event | category | flops | bytes accessed | tf_op | source)
XLA Modules:
  0.0 21.1 jit_solution(10535328419459079558)
XLA Ops:
  0.0 19.7 %shard_map.109 = f32[8,1024]{1,0:T(8,128)} custom-call(bf16[8,16384]{1,0:T(8,128)(2,1)} %amps_hbm.1, bf16[1024,1024]{1,0:T(8,128)(2,1)} %ints_hbm.1, f32[8,1024]{1,0:T(8,128)} %const_hbm.1, s32[2,8]{1,0:T(2,128)} %bitcast.5, s32[2,1024]{1,0:T(2,128)} %bitcast.3, s32[240]{0:T(256)} %occ_irrep_hbm.1, s32[1600]{0:T(1024)} %vir_irrep_hbm.1, f32[240]{0:T(256)} %occ_energy_hbm.1, ...), custom_call_target="tpu_custom_call" | custom-call | flops 268435456 | bytes 2097152 | tf_op jit(solution)/shard_map/pallas_call | solution.py:354
  19.7 1.4 %copy.13 = f32[8,1024]{1,0:T(8,128)} copy(f32[8,1024]{1,0:T(8,128)} %shard_map.109) | data formatting | bytes 65536
